TPU v7x, 256 devices: a whole 4x4x8 slice. The times are simulated.
256 devices in a mesh: dp: 2 (over x_lo), ctx: 128 (over z, y, x_hi, core).
Axes of the slice: x: 4 (x_hi: 2, x_lo: 2; x = x_hi * 2 + x_lo), y: 4, z: 8, core: 2. Of those that a mesh axis runs over, the one named last changes fastest.
Arguments:
- value_rows: bfloat16 [16384, 4096], P('ctx', 'dp'), may hold values from -6 to 6
- gate_rows: bfloat16 [16384, 4096], P('ctx', 'dp'), may hold values from -400 to 400
- filter_rows: bfloat16 [16384, 256], P('ctx', 'dp'), may hold values from -0.046875 to 0.046875
- skip: float32 [4096], P('dp'), may hold values from -4 to 4
- old_owner: int32 [128], replicated, may hold values from 0 to 127, each once
- new_owner: int32 [128], replicated, may hold values from 0 to 127, each once
Outputs:
- mixed_rows: bfloat16 [16384, 4096], P('ctx', 'dp')
Inputs may be any that keep to these rules, and one draw needn't show every extreme that they name: `old_owner`: a permutation of the indices of ctx. `new_owner`: a permutation of the indices of ctx.
All inputs are finite; a program needn't handle non-finite values.
Results may differ from a plain program's by a relative error of at most 0.0095.
Values may be sent and summed in bfloat16 or wider, within the bound.
A program may use at most 64 MiB of HBM per device.

v0:
```python
import functools
import math

import jax
import jax.numpy as jnp
import numpy as np
from jax import lax
from jax.experimental import pallas as pl
from jax.experimental.pallas import tpu as pltpu
from jax.sharding import PartitionSpec as P

MESH = pl.DeviceIdType.MESH
F32 = jnp.float32
BF16 = jnp.bfloat16


def twist(indices, period):
    wrapped = indices % period
    mirror = np.minimum(wrapped, period - wrapped)
    angles = mirror.astype(np.float64) * (2.0 * math.pi / period)
    sines = np.where((mirror == 0) | (2 * mirror == period), 0.0, np.sin(angles))
    sines = np.where(wrapped > period - wrapped, -sines, sines)
    return np.cos(angles), -sines


def make_tables(blocks, rows):
    period, full = 2 * blocks, 2 * blocks * rows
    a, b = np.arange(blocks), np.arange(rows)
    re, im = twist(a[:, None] * a[None, :], period)
    edge = twist(np.full((1, 1), blocks) * a[None, :], period)[0]
    im[:1] = edge
    first = np.concatenate([re, im], axis=0)
    weight = np.full((blocks, 1), 2.0 / full)
    weight[0] = 1.0 / full
    last = np.concatenate([re * weight, im * weight], axis=0)
    turn_re, turn_im = twist(a[:, None] * b[None, :], full)
    edge_re, edge_im = twist(blocks * b[None, :], full)
    dre, dim = twist(b[:, None] * b[None, :], rows)
    fwd = np.block([[dre, dim], [-dim, dre]])
    inv = np.block([[dre, -dim], [dim, dre]])
    low = lambda t: np.asarray(t, np.float32).astype(jnp.bfloat16)
    wide = lambda t: np.asarray(t, np.float32)
    return (
        low(first),
        low(last.T),
        low(fwd),
        low(inv),
        np.stack([wide(turn_re), wide(turn_im)]),
        np.concatenate([wide(edge_re), wide(edge_im)], axis=0),
    )


def transposed(tile):
    return tile.astype(F32).T


def dot(x, y):
    return jnp.dot(x, y, preferred_element_type=F32)


def kernel(
    blocks, group, sizes,
    route_ref, skip_ref, value_ref, gate_ref, filter_ref, old_ref, new_ref,
    first_ref, last_ref, fwd_ref, inv_ref, turn_ref, edge_ref,
    out_ref,
    send_v, send_g, send_f, got_v, got_g, got_f, send_o, got_o,
    wide, lanes, turned, back, conv, edges, sums, partner_sums,
    send_sem, recv_sem,
):
    me = lax.axis_index("ctx")
    half = lax.axis_index("dp")
    rows = value_ref.shape[0]
    channels = value_ref.shape[1]
    per_tile = 128 // group
    nz, ny, nx = sizes

    def peer(k):
        nc = 2
        z = me // (ny * nx * nc)
        y = (me // (nx * nc)) % ny
        x = (me // nc) % nx
        c = me % nc
        dz = k % nz
        r = k // nz
        dy = r % ny
        dx = (r // ny) % nx
        dc = r // (ny * nx)
        return (((z + dz) % nz * ny + (y + dy) % ny) * nx + (x + dx) % nx) * nc + (c + dc) % nc

    barrier = pltpu.get_barrier_semaphore()

    def greet(k, carry):
        pl.semaphore_signal(
            barrier, inc=1, device_id={"ctx": lax.rem(me + k, blocks)}, device_id_type=MESH
        )
        return carry

    lax.fori_loop(1, blocks, greet, 0)
    pl.semaphore_signal(barrier, inc=1, device_id={"dp": 1 - half}, device_id_type=MESH)

    for tile in range(channels // 128):
        at = slice(tile * 128, tile * 128 + 128)
        to = slice(tile * per_tile, tile * per_tile + per_tile)
        send_v[to] = transposed(value_ref[:, at]).astype(BF16).reshape(per_tile, group, rows)
        send_g[to] = transposed(gate_ref[:, at]).astype(BF16).reshape(per_tile, group, rows)
    send_f[...] = transposed(filter_ref[...]).reshape(blocks, 1, rows)
    got_v[me] = send_v[me]
    got_g[me] = send_g[me]
    got_f[me] = send_f[me]

    pl.semaphore_wait(barrier, blocks)

    def remote(src, dst, index, to):
        return pltpu.make_async_remote_copy(
            src_ref=src, dst_ref=dst, send_sem=send_sem.at[index], recv_sem=recv_sem.at[index],
            device_id=to, device_id_type=MESH,
        )

    def all_of(src, dst, index):
        rest = pl.ds(0, blocks - 1)
        return remote(src.at[rest], dst.at[rest], index, {"dp": 1 - half})

    def send_first(k, carry):
        to = peer(k)
        remote(send_v.at[to], got_v.at[me], 0, {"ctx": to}).start()
        remote(send_f.at[to], got_f.at[me], 1, {"ctx": to}).start()
        return carry

    lax.fori_loop(1, blocks, send_first, 0)

    def send_gates(k, carry):
        to = peer(k)
        remote(send_g.at[to], got_g.at[me], 2, {"ctx": to}).start()
        return carry

    lax.fori_loop(1, blocks, send_gates, 0)

    spot = lax.broadcasted_iota(jnp.int32, (blocks, blocks), 0)
    hot_old = jnp.where(old_ref[...] == spot, 1.0, 0.0).astype(BF16)
    hot_new = jnp.where(new_ref[...] == spot, 1.0, 0.0).astype(BF16)
    first_slots = lax.dot_general(
        first_ref[...], hot_old, (((1,), (1,)), ((), ())), preferred_element_type=F32
    ).astype(BF16)
    last_slots = dot(hot_new, last_ref[...]).astype(BF16)

    turn_re, turn_im = turn_ref[0], turn_ref[1]
    edge_re, edge_im = edge_ref[0:1], edge_ref[1:2]
    top = lax.broadcasted_iota(jnp.int32, (blocks, rows), 0) == 0

    def turn(part, unit):
        part = part.astype(BF16).astype(F32)
        re, im = part[:blocks], part[blocks:]
        edges[pl.ds(unit, 1), :] = im[0:1]
        im = jnp.where(top, 0.0, im)
        at = pl.ds(unit * blocks, blocks)
        turned[at, :rows] = (turn_re * re - turn_im * im).astype(BF16)
        turned[at, rows:] = (turn_re * im + turn_im * re).astype(BF16)

    edges[...] = jnp.zeros_like(edges)
    all_of(send_v, got_v, 0).wait_recv()
    wide[...] = got_v[...].astype(F32).reshape(blocks * group, rows)
    for h in range(group):
        lanes[:, h * rows:(h + 1) * rows] = wide[pl.ds(h, blocks, stride=group), :].astype(BF16)
    for h in range(0, group, 2):
        part = dot(first_slots, lanes[:, h * rows:(h + 2) * rows])
        turn(part[:, :rows], h)
        turn(part[:, rows:], h + 1)
    all_of(send_f, got_f, 1).wait_recv()
    taps = got_f[...].reshape(blocks, rows).astype(BF16)
    turn(dot(first_ref[...], taps), group)

    fwd = fwd_ref[...]
    inv = inv_ref[...]
    filt = dot(turned[group * blocks:(group + 1) * blocks], fwd)
    filt_re, filt_im = filt[:, :rows], filt[:, rows:]
    line = edges[...]
    edge_spec = dot(
        jnp.concatenate([(edge_re * line).astype(BF16), (edge_im * line).astype(BF16)], axis=1), fwd
    )

    def multiplied(spec, fre, fim):
        re, im = spec[:, :rows], spec[:, rows:]
        return jnp.concatenate(
            [(re * fre - im * fim).astype(BF16), (re * fim + im * fre).astype(BF16)], axis=1
        )

    edge_filt = edge_spec[group:group + 1]
    edge_inner = dot(multiplied(edge_spec, edge_filt[:, :rows], edge_filt[:, rows:]), inv)
    edges[...] = edge_re * edge_inner[:, :rows] + edge_im * edge_inner[:, rows:]

    for h in range(0, group, 2):
        spec = dot(turned[h * blocks:(h + 2) * blocks], fwd)
        prod = jnp.concatenate(
            [multiplied(spec[:blocks], filt_re, filt_im), multiplied(spec[blocks:], filt_re, filt_im)],
            axis=0,
        )
        inner = dot(prod, inv)
        for i in range(2):
            re = inner[i * blocks:(i + 1) * blocks, :rows]
            im = inner[i * blocks:(i + 1) * blocks, rows:]
            back_im = jnp.where(top, edges[h + i:h + i + 1, :], turn_re * im - turn_im * re)
            at = slice(i * rows, (i + 1) * rows)
            back[:blocks, at] = (turn_re * re + turn_im * im).astype(BF16)
            back[blocks:, at] = back_im.astype(BF16)
        mixed = dot(last_slots, back[...])
        conv[pl.ds(h, blocks, stride=group), :] = mixed[:, :rows]
        conv[pl.ds(h + 1, blocks, stride=group), :] = mixed[:, rows:]

    mine = skip_ref[pl.ds(me, 1), :]
    square = lax.broadcasted_iota(jnp.int32, (group, group), 0) == lax.broadcasted_iota(
        jnp.int32, (group, group), 1
    )
    skips = jnp.sum(jnp.where(square, mine, 0.0), axis=1, keepdims=True)

    all_of(send_g, got_g, 2).wait_recv()

    def gate(to):
        slot = route_ref[to]
        tile = conv[pl.ds(pl.multiple_of(to * group, group), group), :]
        values = got_v[slot].astype(F32)
        return (got_g[slot].astype(F32) * (tile + skips * values)).astype(BF16)

    def send_out(k, carry):
        to = peer(k)
        send_o[to] = gate(to)
        remote(send_o.at[to], got_o.at[me], 3, {"ctx": to}).start()
        return carry

    got_o[me] = gate(me)
    lax.fori_loop(1, blocks, send_out, 0)
    all_of(send_v, got_v, 0).wait_send()
    all_of(send_f, got_f, 1).wait_send()
    all_of(send_g, got_g, 2).wait_send()
    all_of(send_o, got_o, 3).wait_recv()

    full = got_o[...].astype(F32).reshape(blocks * group, rows)
    sums[...] = jnp.broadcast_to(jnp.sum(full * full, axis=0, keepdims=True), sums.shape)
    swap = remote(sums, partner_sums, 4, {"dp": 1 - half})
    swap.start()
    swap.wait()
    scale = lax.rsqrt((sums[0:1] + partner_sums[0:1]) / (2 * channels) + 1e-05)
    for tile in range(channels // 128):
        piece = got_o[tile * per_tile:(tile + 1) * per_tile].astype(F32).reshape(128, rows)
        out_ref[:, tile * 128:(tile + 1) * 128] = (piece * scale).T.astype(BF16)
    all_of(send_o, got_o, 3).wait_send()


def body(sizes, value_rows, gate_rows, filter_rows, skip, old_owner, new_owner):
    blocks = lax.axis_size("ctx")
    rows, channels = value_rows.shape
    group = channels // blocks
    tables = [jnp.asarray(t) for t in make_tables(blocks, rows)]
    lanes = jnp.arange(blocks, dtype=jnp.int32)
    route = jnp.sum(jnp.where(new_owner[:, None] == lanes[None, :], old_owner[:, None], 0), axis=0)
    vmem = pl.BlockSpec(memory_space=pltpu.VMEM)
    smem = pl.BlockSpec(memory_space=pltpu.SMEM)
    slots = pltpu.VMEM((blocks, group, rows), BF16)
    lines = pltpu.VMEM((blocks, 1, rows), F32)
    return pl.pallas_call(
        functools.partial(kernel, blocks, group, sizes),
        out_shape=jax.ShapeDtypeStruct((rows, channels), BF16),
        in_specs=[smem] + [vmem] * 12,
        out_specs=vmem,
        scratch_shapes=[
            slots, slots, lines, slots, slots, lines, slots, slots,
            pltpu.VMEM((blocks * group, rows), F32),
            pltpu.VMEM((blocks, group * rows), BF16),
            pltpu.VMEM(((group + 1) * blocks, 2 * rows), BF16),
            pltpu.VMEM((2 * blocks, 2 * rows), BF16),
            pltpu.VMEM((blocks * group, rows), F32),
            pltpu.VMEM((group + 16, rows), F32),
            pltpu.VMEM((8, rows), F32),
            pltpu.VMEM((8, rows), F32),
            pltpu.SemaphoreType.DMA((5,)),
            pltpu.SemaphoreType.DMA((5,)),
        ],
        compiler_params=pltpu.CompilerParams(
            collective_id=0, has_side_effects=True, vmem_limit_bytes=48 << 20
        ),
    )(
        route, skip.reshape(blocks, group), value_rows, gate_rows, filter_rows,
        old_owner.reshape(1, blocks), new_owner.reshape(1, blocks), *tables,
    )


def solution(mesh):
    placed = (P("ctx", "dp"), P("ctx", "dp"), P("ctx", "dp"), P("dp"), P(), P())
    sizes = (8, 4, 2)
    return jax.shard_map(
        functools.partial(body, sizes), mesh=mesh, in_specs=placed, out_specs=P("ctx", "dp"), check_vma=False
    )
```

profile of v0, /device:TPU:2, one launch (start us, length us, event | category | flops | bytes accessed | tf_op | source)
XLA Modules:
  0.0 71.4 jit_solution(13192934186551390548)
XLA Ops:
  0.0 0.0 copy-start.5
  0.0 0.8 %select_reduce_fusion.route_ref = s32[128]{0:T(128)S(1)} fusion(s32[128]{0:T(128)} %param.16, s32[128]{0:T(128)} %param.17), kind=kLoop, calls=%fused_computation | loop fusion | flops 49024 | bytes 1536 | tf_op jit(solution)/shard_map/reduce_sum | solution.py:254
  0.8 0.0 copy-start.8
  0.8 0.0 copy-start.9
  0.8 0.0 copy-start.10
  0.9 0.8 %reshape.11.skip_ref = f32[128,16]{1,0:T(8,128)S(1)} reshape(f32[2048]{0:T(1024)} %param.15) | data formatting | bytes 16384 | tf_op jit(solution)/shard_map/reshape | solution.py:281
  1.6 0.0 copy-done.5
  1.7 0.0 copy-done.8
  1.7 0.0 copy-done.9
  1.7 0.0 copy-done.10
  1.7 0.0 copy-start
  1.7 1.0 %copy-done = bf16[128,2048]{1,0:T(8,128)(2,1)S(1)} copy-done((bf16[128,2048]{1,0:T(8,128)(2,1)S(1)}, bf16[128,2048]{1,0:T(8,128)(2,1)}, u32[]{:S(2)}) %copy-start) | copy-done | bytes 524312
  2.7 0.0 copy-start.1
  2.7 1.0 %copy-done.1 = bf16[128,2048]{1,0:T(8,128)(2,1)S(1)} copy-done((bf16[128,2048]{1,0:T(8,128)(2,1)S(1)}, bf16[128,2048]{1,0:T(8,128)(2,1)}, u32[]{:S(2)}) %copy-start.1) | copy-done | bytes 524312
  3.8 0.0 copy-start.2
  3.8 0.9 %copy-done.2 = f32[2,128,128]{2,1,0:T(8,128)S(1)} copy-done((f32[2,128,128]{2,1,0:T(8,128)S(1)}, f32[2,128,128]{2,1,0:T(8,128)}, u32[]{:S(2)}) %copy-start.2) | copy-done | bytes 131096
  4.7 0.0 copy-start.3
  4.7 0.9 %copy-done.3 = bf16[256,256]{1,0:T(8,128)(2,1)S(1)} copy-done((bf16[256,256]{1,0:T(8,128)(2,1)S(1)}, bf16[256,256]{1,0:T(8,128)(2,1)}, u32[]{:S(2)}) %copy-start.3) | copy-done | bytes 131096
  5.6 0.0 copy-start.4
  5.6 0.9 %copy-done.4 = bf16[256,256]{1,0:T(8,128)(2,1)S(1)} copy-done((bf16[256,256]{1,0:T(8,128)(2,1)S(1)}, bf16[256,256]{1,0:T(8,128)(2,1)}, u32[]{:S(2)}) %copy-start.4) | copy-done | bytes 131096
  6.5 0.0 copy-start.6
  6.5 0.8 %copy-done.6 = bf16[256,128]{1,0:T(8,128)(2,1)S(1)} copy-done((bf16[256,128]{1,0:T(8,128)(2,1)S(1)}, bf16[256,128]{1,0:T(8,128)(2,1)}, u32[]{:S(2)}) %copy-start.6) | copy-done | bytes 65560
  7.3 0.0 copy-start.7
  7.3 0.8 %copy-done.7 = bf16[128,128]{1,0:T(8,128)(2,1)S(1)} copy-done((bf16[128,128]{1,0:T(8,128)(2,1)S(1)}, bf16[128,128]{1,0:T(8,128)(2,1)}, u32[]{:S(2)}) %copy-start.7) | copy-done | bytes 32792
  8.1 62.5 %shard_map.118 = bf16[128,2048]{1,0:T(8,128)(2,1)S(1)} custom-call(s32[128]{0:T(128)S(1)} %select_reduce_fusion.route_ref, f32[128,16]{1,0:T(8,128)S(1)} %reshape.11.skip_ref, bf16[128,2048]{1,0:T(8,128)(2,1)S(1)} %copy-done, bf16[128,2048]{1,0:T(8,128)(2,1)S(1)} %copy-done.1, bf16[128,128]{1,0:T(8,128)(2,1)S(1)} %copy-done.7, s32[1,128]{1,0:T(1,128)S(1)} %bitcast.2, ...), custom_call_target="tpu_custom_call" | custom-call | tf_op jit(solution)/shard_map/pallas_call | solution.py:259
  70.6 0.8 %copy.14 = bf16[128,2048]{1,0:T(8,128)(2,1)} copy(bf16[128,2048]{1,0:T(8,128)(2,1)S(1)} %shard_map.118) | data formatting | bytes 1048576
Async XLA Ops:
  0.0 1.6 %copy-start.5 = (bf16[128,256]{1,0:T(8,128)(2,1)S(1)}, bf16[128,256]{1,0:T(8,128)(2,1)}, u32[]{:S(2)}) copy-start(bf16[128,256]{1,0:T(8,128)(2,1)} %constant.15.clone.last_ref) | copy-start | bytes 196612
  0.8 0.8 %copy-start.8 = (f32[2,128]{1,0:T(2,128)S(1)}, f32[2,128]{1,0:T(2,128)}, u32[]{:S(2)}) copy-start(f32[2,128]{1,0:T(2,128)} %constant.19.clone.edge_ref) | copy-start | bytes 3076
  0.8 0.8 %copy-start.9 = (s32[128]{0:T(128)S(1)}, s32[128]{0:T(128)}, u32[]{:S(2)}) copy-start(s32[128]{0:T(128)} %param.16) | copy-start | bytes 1540
  0.8 0.8 %copy-start.10 = (s32[128]{0:T(128)S(1)}, s32[128]{0:T(128)}, u32[]{:S(2)}) copy-start(s32[128]{0:T(128)} %param.17) | copy-start | bytes 1540
  1.7 1.0 %copy-start = (bf16[128,2048]{1,0:T(8,128)(2,1)S(1)}, bf16[128,2048]{1,0:T(8,128)(2,1)}, u32[]{:S(2)}) copy-start(bf16[128,2048]{1,0:T(8,128)(2,1)} %value_ref.1) | copy-start | bytes 1572868
  2.7 1.0 %copy-start.1 = (bf16[128,2048]{1,0:T(8,128)(2,1)S(1)}, bf16[128,2048]{1,0:T(8,128)(2,1)}, u32[]{:S(2)}) copy-start(bf16[128,2048]{1,0:T(8,128)(2,1)} %gate_ref.1) | copy-start | bytes 1572868
  3.8 0.9 %copy-start.2 = (f32[2,128,128]{2,1,0:T(8,128)S(1)}, f32[2,128,128]{2,1,0:T(8,128)}, u32[]{:S(2)}) copy-start(f32[2,128,128]{2,1,0:T(8,128)} %constant.18.clone.turn_ref) | copy-start | bytes 393220
  4.7 0.9 %copy-start.3 = (bf16[256,256]{1,0:T(8,128)(2,1)S(1)}, bf16[256,256]{1,0:T(8,128)(2,1)}, u32[]{:S(2)}) copy-start(bf16[256,256]{1,0:T(8,128)(2,1)} %constant.17.clone.inv_ref) | copy-start | bytes 393220
  5.6 0.9 %copy-start.4 = (bf16[256,256]{1,0:T(8,128)(2,1)S(1)}, bf16[256,256]{1,0:T(8,128)(2,1)}, u32[]{:S(2)}) copy-start(bf16[256,256]{1,0:T(8,128)(2,1)} %constant.16.clone.fwd_ref) | copy-start | bytes 393220
  6.5 0.8 %copy-start.6 = (bf16[256,128]{1,0:T(8,128)(2,1)S(1)}, bf16[256,128]{1,0:T(8,128)(2,1)}, u32[]{:S(2)}) copy-start(bf16[256,128]{1,0:T(8,128)(2,1)} %constant.14.clone.first_ref) | copy-start | bytes 196612
  7.3 0.8 %copy-start.7 = (bf16[128,128]{1,0:T(8,128)(2,1)S(1)}, bf16[128,128]{1,0:T(8,128)(2,1)}, u32[]{:S(2)}) copy-start(bf16[128,128]{1,0:T(8,128)(2,1)} %filter_ref.1) | copy-start | bytes 98308
where the time goes:
time: 72.1 us; the launch traced here: 71.4 us
  Pallas kernels  62.5 us (87%)
  local copies, waits for them, and re-layouts  7.99 us (11%)
  other arithmetic  0.81 us (1%)
    pallas_call x1, Pallas kernels, body(): pl.pallas_call(functools.partial(kernel, blocks, group, sizes), out_shape...  62.5 us
    unnamed x23, local copies, waits for them, and re-layouts  7.2 us

commit v1 on v0

--- a/solution.py
+++ b/solution.py
@@ -42,9 +42,9 @@
     wide = lambda t: np.asarray(t, np.float32)
     return (
         low(first),
-        low(last.T),
-        low(fwd),
-        low(inv),
+        low(np.concatenate([last[:blocks].T, last[blocks:].T], axis=0)),
+        low(np.concatenate([fwd[:, :rows], fwd[:, rows:]], axis=0)),
+        low(np.concatenate([inv[:, :rows], inv[:, rows:]], axis=0)),
         np.stack([wide(turn_re), wide(turn_im)]),
         np.concatenate([wide(edge_re), wide(edge_im)], axis=0),
     )
@@ -54,38 +54,43 @@
     return tile.astype(F32).T
 
 
+def beside(ref):
+    depth = ref.shape[0] // 2
+    return jnp.concatenate([ref[:depth], ref[depth:]], axis=1)
+
+
 def dot(x, y):
     return jnp.dot(x, y, preferred_element_type=F32)
 
 
 def kernel(
     blocks, group, sizes,
-    route_ref, skip_ref, value_ref, gate_ref, filter_ref, old_ref, new_ref,
+    skip_ref, value_hbm, gate_hbm, filter_hbm, old_hbm, new_hbm,
+    first_hbm, last_hbm, fwd_hbm, inv_hbm, turn_hbm, edge_hbm,
+    out_hbm, scale_ref, out_ref,
+    value_ref, gate_ref, filter_ref, old_ref, new_ref,
     first_ref, last_ref, fwd_ref, inv_ref, turn_ref, edge_ref,
-    out_ref,
     send_v, send_g, send_f, got_v, got_g, got_f, send_o, got_o,
-    wide, lanes, turned, back, conv, edges, sums, partner_sums,
-    send_sem, recv_sem,
+    wide, lanes, turned, back, conv, edges, sums, partner_sums, route_row, route_ref,
+    load_sem, send_sem, recv_sem,
 ):
     me = lax.axis_index("ctx")
     half = lax.axis_index("dp")
-    rows = value_ref.shape[0]
-    channels = value_ref.shape[1]
+    rows, channels = value_ref.shape
     per_tile = 128 // group
-    nz, ny, nx = sizes
-
-    def peer(k):
-        nc = 2
-        z = me // (ny * nx * nc)
-        y = (me // (nx * nc)) % ny
-        x = (me // nc) % nx
-        c = me % nc
-        dz = k % nz
-        r = k // nz
-        dy = r % ny
-        dx = (r // ny) % nx
-        dc = r // (ny * nx)
-        return (((z + dz) % nz * ny + (y + dy) % ny) * nx + (x + dx) % nx) * nc + (c + dc) % nc
+    nz, ny, nx, nc = sizes
+    low = ny * nx * nc
+
+    loads = [
+        pltpu.make_async_copy(src, dst, load_sem.at[i])
+        for i, (src, dst) in enumerate([
+            (value_hbm, value_ref), (filter_hbm, filter_ref), (gate_hbm, gate_ref),
+            (old_hbm, old_ref), (new_hbm, new_ref), (first_hbm, first_ref), (last_hbm, last_ref),
+            (turn_hbm, turn_ref), (edge_hbm, edge_ref), (fwd_hbm, fwd_ref), (inv_hbm, inv_ref),
+        ])
+    ]
+    for load in loads:
+        load.start()
 
     barrier = pltpu.get_barrier_semaphore()
 
@@ -95,20 +100,26 @@
         )
         return carry
 
-    lax.fori_loop(1, blocks, greet, 0)
+    lax.fori_loop(1, blocks, greet, 0, unroll=8)
     pl.semaphore_signal(barrier, inc=1, device_id={"dp": 1 - half}, device_id_type=MESH)
 
-    for tile in range(channels // 128):
-        at = slice(tile * 128, tile * 128 + 128)
-        to = slice(tile * per_tile, tile * per_tile + per_tile)
-        send_v[to] = transposed(value_ref[:, at]).astype(BF16).reshape(per_tile, group, rows)
-        send_g[to] = transposed(gate_ref[:, at]).astype(BF16).reshape(per_tile, group, rows)
-    send_f[...] = transposed(filter_ref[...]).reshape(blocks, 1, rows)
-    got_v[me] = send_v[me]
-    got_g[me] = send_g[me]
-    got_f[me] = send_f[me]
-
-    pl.semaphore_wait(barrier, blocks)
+    z, y, x, c = me // low, (me // (nx * nc)) % ny, (me // nc) % nx, me % nc
+    heights = [((z + dz) % nz) * low for dz in range(nz)]
+
+    def each_peer(act):
+        for dz in range(1, nz):
+            act(heights[dz] + me % low)
+
+        def turn_of(r, carry):
+            dy = r % ny
+            dx = (r // ny) % nx
+            dc = r // (ny * nx)
+            place = (((y + dy) % ny) * nx + (x + dx) % nx) * nc + (c + dc) % nc
+            for dz in range(nz):
+                act(heights[dz] + place)
+            return carry
+
+        lax.fori_loop(1, low, turn_of, 0)
 
     def remote(src, dst, index, to):
         return pltpu.make_async_remote_copy(
@@ -120,20 +131,34 @@
         rest = pl.ds(0, blocks - 1)
         return remote(src.at[rest], dst.at[rest], index, {"dp": 1 - half})
 
-    def send_first(k, carry):
-        to = peer(k)
+    def prepare(ref, send):
+        for tile in range(channels // 128):
+            to = slice(tile * per_tile, tile * per_tile + per_tile)
+            piece = transposed(ref[:, tile * 128:(tile + 1) * 128])
+            send[to] = piece.astype(BF16).reshape(per_tile, group, rows)
+
+    loads[0].wait()
+    prepare(value_ref, send_v)
+    got_v[me] = send_v[me]
+    loads[1].wait()
+    send_f[...] = transposed(filter_ref[...]).reshape(blocks, 1, rows)
+    got_f[me] = send_f[me]
+
+    pl.semaphore_wait(barrier, blocks)
+
+    def send_first(to):
         remote(send_v.at[to], got_v.at[me], 0, {"ctx": to}).start()
         remote(send_f.at[to], got_f.at[me], 1, {"ctx": to}).start()
-        return carry
-
-    lax.fori_loop(1, blocks, send_first, 0)
-
-    def send_gates(k, carry):
-        to = peer(k)
-        remote(send_g.at[to], got_g.at[me], 2, {"ctx": to}).start()
-        return carry
-
-    lax.fori_loop(1, blocks, send_gates, 0)
+
+    each_peer(send_first)
+
+    loads[2].wait()
+    prepare(gate_ref, send_g)
+    got_g[me] = send_g[me]
+    each_peer(lambda to: remote(send_g.at[to], got_g.at[me], 2, {"ctx": to}).start())
+
+    for load in loads[3:]:
+        load.wait()
 
     spot = lax.broadcasted_iota(jnp.int32, (blocks, blocks), 0)
     hot_old = jnp.where(old_ref[...] == spot, 1.0, 0.0).astype(BF16)
@@ -141,7 +166,14 @@
     first_slots = lax.dot_general(
         first_ref[...], hot_old, (((1,), (1,)), ((), ())), preferred_element_type=F32
     ).astype(BF16)
-    last_slots = dot(hot_new, last_ref[...]).astype(BF16)
+    last_slots = dot(hot_new, beside(last_ref)).astype(BF16)
+
+    column = jnp.sum(jnp.where(new_ref[...] == spot, old_ref[...], 0), axis=1, keepdims=True)
+    other = lax.broadcasted_iota(jnp.int32, (blocks, blocks), 1)
+    row = jnp.sum(jnp.where(spot == other, column, 0), axis=0, keepdims=True)
+    route_row[...] = jnp.broadcast_to(row, route_row.shape)
+    routed = pltpu.make_async_copy(route_row, route_ref, load_sem.at[len(loads)])
+    routed.start()
 
     turn_re, turn_im = turn_ref[0], turn_ref[1]
     edge_re, edge_im = edge_ref[0:1], edge_ref[1:2]
@@ -169,8 +201,8 @@
     taps = got_f[...].reshape(blocks, rows).astype(BF16)
     turn(dot(first_ref[...], taps), group)
 
-    fwd = fwd_ref[...]
-    inv = inv_ref[...]
+    fwd = beside(fwd_ref)
+    inv = beside(inv_ref)
     filt = dot(turned[group * blocks:(group + 1) * blocks], fwd)
     filt_re, filt_im = filt[:, :rows], filt[:, rows:]
     line = edges[...]
@@ -206,28 +238,26 @@
         conv[pl.ds(h, blocks, stride=group), :] = mixed[:, :rows]
         conv[pl.ds(h + 1, blocks, stride=group), :] = mixed[:, rows:]
 
-    mine = skip_ref[pl.ds(me, 1), :]
-    square = lax.broadcasted_iota(jnp.int32, (group, group), 0) == lax.broadcasted_iota(
-        jnp.int32, (group, group), 1
-    )
-    skips = jnp.sum(jnp.where(square, mine, 0.0), axis=1, keepdims=True)
-
+    sublane = lax.broadcasted_iota(jnp.int32, (group, rows), 0)
+    skips = jnp.zeros((group, rows), F32)
+    for h in range(group):
+        skips = jnp.where(sublane == h, skip_ref[me * group + h], skips)
+
+    routed.wait()
     all_of(send_g, got_g, 2).wait_recv()
 
     def gate(to):
-        slot = route_ref[to]
+        slot = route_ref[0, to]
         tile = conv[pl.ds(pl.multiple_of(to * group, group), group), :]
         values = got_v[slot].astype(F32)
         return (got_g[slot].astype(F32) * (tile + skips * values)).astype(BF16)
 
-    def send_out(k, carry):
-        to = peer(k)
+    def send_out(to):
         send_o[to] = gate(to)
         remote(send_o.at[to], got_o.at[me], 3, {"ctx": to}).start()
-        return carry
 
     got_o[me] = gate(me)
-    lax.fori_loop(1, blocks, send_out, 0)
+    each_peer(send_out)
     all_of(send_v, got_v, 0).wait_send()
     all_of(send_f, got_f, 1).wait_send()
     all_of(send_g, got_g, 2).wait_send()
@@ -237,11 +267,14 @@
     sums[...] = jnp.broadcast_to(jnp.sum(full * full, axis=0, keepdims=True), sums.shape)
     swap = remote(sums, partner_sums, 4, {"dp": 1 - half})
     swap.start()
+    for tile in range(channels // 128):
+        piece = got_o[tile * per_tile:(tile + 1) * per_tile].reshape(128, rows)
+        out_ref[:, tile * 128:(tile + 1) * 128] = transposed(piece).astype(BF16)
+    store = pltpu.make_async_copy(out_ref, out_hbm, load_sem.at[len(loads) + 1])
+    store.start()
     swap.wait()
-    scale = lax.rsqrt((sums[0:1] + partner_sums[0:1]) / (2 * channels) + 1e-05)
-    for tile in range(channels // 128):
-        piece = got_o[tile * per_tile:(tile + 1) * per_tile].astype(F32).reshape(128, rows)
-        out_ref[:, tile * 128:(tile + 1) * 128] = (piece * scale).T.astype(BF16)
+    scale_ref[...] = lax.rsqrt((sums[0:1] + partner_sums[0:1]) / (2 * channels) + 1e-05)
+    store.wait()
     all_of(send_o, got_o, 3).wait_send()
 
 
@@ -250,18 +283,23 @@
     rows, channels = value_rows.shape
     group = channels // blocks
     tables = [jnp.asarray(t) for t in make_tables(blocks, rows)]
-    lanes = jnp.arange(blocks, dtype=jnp.int32)
-    route = jnp.sum(jnp.where(new_owner[:, None] == lanes[None, :], old_owner[:, None], 0), axis=0)
+    hbm = pl.BlockSpec(memory_space=pltpu.HBM)
     vmem = pl.BlockSpec(memory_space=pltpu.VMEM)
     smem = pl.BlockSpec(memory_space=pltpu.SMEM)
     slots = pltpu.VMEM((blocks, group, rows), BF16)
     lines = pltpu.VMEM((blocks, 1, rows), F32)
-    return pl.pallas_call(
+    owners = (old_owner.reshape(1, blocks), new_owner.reshape(1, blocks))
+    arrays = (value_rows, gate_rows, filter_rows, *owners, *tables)
+    loaded = [pltpu.VMEM(t.shape, t.dtype) for t in arrays]
+    mixed, scale = pl.pallas_call(
         functools.partial(kernel, blocks, group, sizes),
-        out_shape=jax.ShapeDtypeStruct((rows, channels), BF16),
-        in_specs=[smem] + [vmem] * 12,
-        out_specs=vmem,
-        scratch_shapes=[
+        out_shape=[
+            jax.ShapeDtypeStruct((rows, channels), BF16),
+            jax.ShapeDtypeStruct((1, rows), F32),
+        ],
+        in_specs=[smem] + [hbm] * len(arrays),
+        out_specs=[hbm, vmem],
+        scratch_shapes=[pltpu.VMEM((rows, channels), BF16)] + loaded + [
             slots, slots, lines, slots, slots, lines, slots, slots,
             pltpu.VMEM((blocks * group, rows), F32),
             pltpu.VMEM((blocks, group * rows), BF16),
@@ -271,21 +309,22 @@
             pltpu.VMEM((group + 16, rows), F32),
             pltpu.VMEM((8, rows), F32),
             pltpu.VMEM((8, rows), F32),
+            pltpu.VMEM((8, blocks), jnp.int32),
+            pltpu.SMEM((8, blocks), jnp.int32),
+            pltpu.SemaphoreType.DMA((len(arrays) + 2,)),
             pltpu.SemaphoreType.DMA((5,)),
             pltpu.SemaphoreType.DMA((5,)),
         ],
         compiler_params=pltpu.CompilerParams(
-            collective_id=0, has_side_effects=True, vmem_limit_bytes=48 << 20
+            collective_id=0, has_side_effects=True, vmem_limit_bytes=64 << 20
         ),
-    )(
-        route, skip.reshape(blocks, group), value_rows, gate_rows, filter_rows,
-        old_owner.reshape(1, blocks), new_owner.reshape(1, blocks), *tables,
-    )
+    )(skip, *arrays)
+    return (mixed.astype(F32) * scale.reshape(rows, 1)).astype(BF16)
 
 
 def solution(mesh):
     placed = (P("ctx", "dp"), P("ctx", "dp"), P("ctx", "dp"), P("dp"), P(), P())
-    sizes = (8, 4, 2)
+    sizes = (8, 4, 2, 2)
     return jax.shard_map(
         functools.partial(body, sizes), mesh=mesh, in_specs=placed, out_specs=P("ctx", "dp"), check_vma=False
     )

time: 72.1 us -> 66.2 us (0.918)
  local copies, waits for them, and re-layouts: 7.99 us -> 0.66 us
  other arithmetic: 0.81 us -> 1.99 us
    unnamed x23 -> x2, local copies, waits for them, and re-layouts: 7.2 us -> 0.66 us
    convert_element_type x0 -> x1, other arithmetic: none -> 1.99 us  [body(): return (mixed.astype(F32) * scale.reshape(rows, 1)).astype(BF16)]
    reduce_sum x1 -> x0, other arithmetic: 0.81 us -> none  [body(): jnp.sum(jnp.where(new_owner[:, None] == lanes[None, :], old_owner[:, None...]
    reshape x1 -> x0, local copies, waits for them, and re-layouts: 0.79 us -> none  [body(): skip.reshape(blocks, group)]
where the time goes in v1:
time: 66.2 us; the launch traced here: 65.7 us
  Pallas kernels  63.1 us (95%)
  other arithmetic  1.99 us (3%)
    pallas_call x1, Pallas kernels, body(): pl.pallas_call(functools.partial(kernel, blocks, group, sizes), out_shape...  63.1 us
    convert_element_type x1, other arithmetic, body(): return (mixed.astype(F32) * scale.reshape(rows, 1)).astype(BF16)  1.99 us

profile of v1, /device:TPU:2, one launch (start us, length us, event | category | flops | bytes accessed | tf_op | source)
XLA Modules:
  0.0 65.7 jit_solution(16925212034386994610)
XLA Ops:
  0.0 63.1 %shard_map.118 = (bf16[128,2048]{1,0:T(8,128)(2,1)}, f32[1,128]{1,0:T(1,128)}) custom-call(f32[2048]{0:T(1024)} %skip_ref.1, bf16[128,2048]{1,0:T(8,128)(2,1)} %value_hbm.1, bf16[128,2048]{1,0:T(8,128)(2,1)} %gate_hbm.1, bf16[128,128]{1,0:T(8,128)(2,1)} %filter_hbm.1, s32[1,128]{1,0:T(1,128)} %bitcast.3, s32[1,128]{1,0:T(1,128)} %bitcast.4, ...), custom_call_target="tpu_custom_call" | custom-call | tf_op jit(solution)/shard_map/pallas_call | solution.py:294
  63.1 0.0 copy-start
  63.1 0.7 %copy-done = f32[1,128]{1,0:T(1,128)S(1)} copy-done((f32[1,128]{1,0:T(1,128)S(1)}, f32[1,128]{1,0:T(1,128)}, u32[]{:S(2)}) %copy-start) | copy-done | bytes 536
  63.7 2.0 %multiply_convert_fusion = bf16[128,2048]{1,0:T(8,128)(2,1)} fusion(bf16[128,2048]{1,0:T(8,128)(2,1)} %get-tuple-element.7, f32[128]{0:T(128)S(1)} %bitcast.5), kind=kLoop, calls=%fused_computation | loop fusion | flops 786432 | bytes 1049088 | tf_op jit(solution)/shard_map/convert_element_type | solution.py:322
Async XLA Ops:
  63.1 0.7 %copy-start = (f32[1,128]{1,0:T(1,128)S(1)}, f32[1,128]{1,0:T(1,128)}, u32[]{:S(2)}) copy-start(f32[1,128]{1,0:T(1,128)} %get-tuple-element.8) | copy-start | bytes 1540

commit v2 on v1

--- a/solution.py
+++ b/solution.py
@@ -67,7 +67,7 @@
     blocks, group, sizes,
     skip_ref, value_hbm, gate_hbm, filter_hbm, old_hbm, new_hbm,
     first_hbm, last_hbm, fwd_hbm, inv_hbm, turn_hbm, edge_hbm,
-    out_hbm, scale_ref, out_ref,
+    out_hbm, out_ref,
     value_ref, gate_ref, filter_ref, old_ref, new_ref,
     first_ref, last_ref, fwd_ref, inv_ref, turn_ref, edge_ref,
     send_v, send_g, send_f, got_v, got_g, got_f, send_o, got_o,
@@ -107,19 +107,21 @@
     heights = [((z + dz) % nz) * low for dz in range(nz)]
 
     def each_peer(act):
-        for dz in range(1, nz):
-            act(heights[dz] + me % low)
-
-        def turn_of(r, carry):
+        steps = (4, 3, 5, 2, 6, 1, 7, 0)
+
+        def turn_of(i, carry):
+            r = low - 1 - i
             dy = r % ny
             dx = (r // ny) % nx
             dc = r // (ny * nx)
             place = (((y + dy) % ny) * nx + (x + dx) % nx) * nc + (c + dc) % nc
-            for dz in range(nz):
+            for dz in steps:
                 act(heights[dz] + place)
             return carry
 
-        lax.fori_loop(1, low, turn_of, 0)
+        lax.fori_loop(0, low - 1, turn_of, 0)
+        for dz in steps[:-1]:
+            act(heights[dz] + me % low)
 
     def remote(src, dst, index, to):
         return pltpu.make_async_remote_copy(
@@ -270,11 +272,18 @@
     for tile in range(channels // 128):
         piece = got_o[tile * per_tile:(tile + 1) * per_tile].reshape(128, rows)
         out_ref[:, tile * 128:(tile + 1) * 128] = transposed(piece).astype(BF16)
-    store = pltpu.make_async_copy(out_ref, out_hbm, load_sem.at[len(loads) + 1])
-    store.start()
     swap.wait()
-    scale_ref[...] = lax.rsqrt((sums[0:1] + partner_sums[0:1]) / (2 * channels) + 1e-05)
-    store.wait()
+    scale = lax.rsqrt((sums[...] + partner_sums[...]) / (2 * channels) + 1e-05).T[:, 0:1]
+    stores = []
+    for i in range(4):
+        at = slice(i * (channels // 4), (i + 1) * (channels // 4))
+        out_ref[:, at] = (out_ref[:, at].astype(F32) * scale).astype(BF16)
+        stores.append(
+            pltpu.make_async_copy(out_ref.at[:, at], out_hbm.at[:, at], load_sem.at[len(loads) + 1 + i])
+        )
+        stores[-1].start()
+    for store in stores:
+        store.wait()
     all_of(send_o, got_o, 3).wait_send()
 
 
@@ -284,21 +293,17 @@
     group = channels // blocks
     tables = [jnp.asarray(t) for t in make_tables(blocks, rows)]
     hbm = pl.BlockSpec(memory_space=pltpu.HBM)
-    vmem = pl.BlockSpec(memory_space=pltpu.VMEM)
     smem = pl.BlockSpec(memory_space=pltpu.SMEM)
     slots = pltpu.VMEM((blocks, group, rows), BF16)
     lines = pltpu.VMEM((blocks, 1, rows), F32)
     owners = (old_owner.reshape(1, blocks), new_owner.reshape(1, blocks))
     arrays = (value_rows, gate_rows, filter_rows, *owners, *tables)
     loaded = [pltpu.VMEM(t.shape, t.dtype) for t in arrays]
-    mixed, scale = pl.pallas_call(
+    return pl.pallas_call(
         functools.partial(kernel, blocks, group, sizes),
-        out_shape=[
-            jax.ShapeDtypeStruct((rows, channels), BF16),
-            jax.ShapeDtypeStruct((1, rows), F32),
-        ],
+        out_shape=jax.ShapeDtypeStruct((rows, channels), BF16),
         in_specs=[smem] + [hbm] * len(arrays),
-        out_specs=[hbm, vmem],
+        out_specs=hbm,
         scratch_shapes=[pltpu.VMEM((rows, channels), BF16)] + loaded + [
             slots, slots, lines, slots, slots, lines, slots, slots,
             pltpu.VMEM((blocks * group, rows), F32),
@@ -311,7 +316,7 @@
             pltpu.VMEM((8, rows), F32),
             pltpu.VMEM((8, blocks), jnp.int32),
             pltpu.SMEM((8, blocks), jnp.int32),
-            pltpu.SemaphoreType.DMA((len(arrays) + 2,)),
+            pltpu.SemaphoreType.DMA((len(arrays) + 5,)),
             pltpu.SemaphoreType.DMA((5,)),
             pltpu.SemaphoreType.DMA((5,)),
         ],
@@ -319,7 +324,6 @@
             collective_id=0, has_side_effects=True, vmem_limit_bytes=64 << 20
         ),
     )(skip, *arrays)
-    return (mixed.astype(F32) * scale.reshape(rows, 1)).astype(BF16)
 
 
 def solution(mesh):

time: 66.2 us -> 61.6 us (0.931)
  Pallas kernels: 63.1 us -> 59.5 us
  other arithmetic: 1.99 us -> 0 us
  local copies, waits for them, and re-layouts: 0.66 us -> 1.88 us
    pallas_call x1, Pallas kernels: 63.1 us -> 59.5 us  [body(): pl.pallas_call(functools.partial(kernel, blocks, group, sizes), out_shape...]
    convert_element_type x1 -> x0, other arithmetic: 1.99 us -> none  [body(): return (mixed.astype(F32) * scale.reshape(rows, 1)).astype(BF16)]
    unnamed x2 -> x1, local copies, waits for them, and re-layouts: 0.66 us -> 1.88 us
where the time goes in v2:
time: 61.6 us; the launch traced here: 61.4 us
  Pallas kernels  59.5 us (97%)
  local copies, waits for them, and re-layouts  1.88 us (3%)
    pallas_call x1, Pallas kernels, body(): pl.pallas_call(functools.partial(kernel, blocks, group, sizes), out_shape...  59.5 us
    unnamed x1, local copies, waits for them, and re-layouts  1.88 us

profile of v2, /device:TPU:2, one launch (start us, length us, event | category | flops | bytes accessed | tf_op | source)
XLA Modules:
  0.0 61.4 jit_solution(622574099198202303)
XLA Ops:
  0.0 59.5 %shard_map.118 = bf16[128,2048]{1,0:T(8,128)(2,1)} custom-call(f32[2048]{0:T(1024)} %skip_ref.1, bf16[128,2048]{1,0:T(8,128)(2,1)} %value_hbm.1, bf16[128,2048]{1,0:T(8,128)(2,1)} %gate_hbm.1, bf16[128,128]{1,0:T(8,128)(2,1)} %filter_hbm.1, s32[1,128]{1,0:T(1,128)} %bitcast.2, s32[1,128]{1,0:T(1,128)} %bitcast.3, bf16[256,128]{1,0:T(8,128)(2,1)} %constant.12.clone.first_hbm, ...), custom_call_target="tpu_custom_call" | custom-call | tf_op jit(solution)/shard_map/pallas_call | solution.py:302
  59.5 1.9 %copy.14 = bf16[128,2048]{1,0:T(8,128)(2,1)} copy(bf16[128,2048]{1,0:T(8,128)(2,1)} %shard_map.118) | data formatting | bytes 1048576

commit v3 on v2

--- a/solution.py
+++ b/solution.py
@@ -70,7 +70,7 @@
     out_hbm, out_ref,
     value_ref, gate_ref, filter_ref, old_ref, new_ref,
     first_ref, last_ref, fwd_ref, inv_ref, turn_ref, edge_ref,
-    send_v, send_g, send_f, got_v, got_g, got_f, send_o, got_o,
+    send_v, send_g, got_v, got_g, send_o, got_o, send_f, got_f, send_f2, got_f2,
     wide, lanes, turned, back, conv, edges, sums, partner_sums, route_row, route_ref,
     load_sem, send_sem, recv_sem,
 ):
@@ -143,20 +143,38 @@
     prepare(value_ref, send_v)
     got_v[me] = send_v[me]
     loads[1].wait()
-    send_f[...] = transposed(filter_ref[...]).reshape(blocks, 1, rows)
-    got_f[me] = send_f[me]
+    here = me % low
+    wide[:blocks] = transposed(filter_ref[...])
+    for place in range(low):
+        send_f[place * nz:(place + 1) * nz] = wide[pl.ds(place, nz, stride=low), :]
+
+    def of_place(ref, place):
+        return ref.at[pl.ds(pl.multiple_of(place * nz, nz), nz)]
+
+    own = pl.ds(pl.multiple_of(here * nz, nz), nz)
+    got_f[own, :] = send_f[own, :]
 
     pl.semaphore_wait(barrier, blocks)
 
-    def send_first(to):
-        remote(send_v.at[to], got_v.at[me], 0, {"ctx": to}).start()
-        remote(send_f.at[to], got_f.at[me], 1, {"ctx": to}).start()
-
-    each_peer(send_first)
+    for step in range(1, low):
+        place = (here + step) % low
+        remote(of_place(send_f, place), of_place(got_f, here), 1, {"ctx": z * low + place}).start()
+    each_peer(lambda to: remote(send_v.at[to], got_v.at[me], 0, {"ctx": to}).start())
 
     loads[2].wait()
     prepare(gate_ref, send_g)
     got_g[me] = send_g[me]
+    rest = pl.ds(0, (low - 1) * nz)
+    first_hop = remote(send_f.at[rest], got_f.at[rest], 1, {"dp": 1 - half})
+    first_hop.wait_recv()
+    for height in range(nz):
+        send_f2[height] = got_f[pl.ds(height, low, stride=nz), :].astype(BF16)
+    got_f2[z] = send_f2[z]
+    for dz in range(1, nz):
+        height = (z + dz) % nz
+        remote(send_f2.at[height], got_f2.at[z], 5, {"ctx": height * low + here}).start()
+    rest = pl.ds(0, nz - 1)
+    second_hop = remote(send_f2.at[rest], got_f2.at[rest], 5, {"dp": 1 - half})
     each_peer(lambda to: remote(send_g.at[to], got_g.at[me], 2, {"ctx": to}).start())
 
     for load in loads[3:]:
@@ -199,8 +217,8 @@
         part = dot(first_slots, lanes[:, h * rows:(h + 2) * rows])
         turn(part[:, :rows], h)
         turn(part[:, rows:], h + 1)
-    all_of(send_f, got_f, 1).wait_recv()
-    taps = got_f[...].reshape(blocks, rows).astype(BF16)
+    second_hop.wait_recv()
+    taps = got_f2[...].reshape(blocks, rows)
     turn(dot(first_ref[...], taps), group)
 
     fwd = beside(fwd_ref)
@@ -260,9 +278,6 @@
 
     got_o[me] = gate(me)
     each_peer(send_out)
-    all_of(send_v, got_v, 0).wait_send()
-    all_of(send_f, got_f, 1).wait_send()
-    all_of(send_g, got_g, 2).wait_send()
     all_of(send_o, got_o, 3).wait_recv()
 
     full = got_o[...].astype(F32).reshape(blocks * group, rows)
@@ -284,6 +299,10 @@
         stores[-1].start()
     for store in stores:
         store.wait()
+    all_of(send_v, got_v, 0).wait_send()
+    first_hop.wait_send()
+    second_hop.wait_send()
+    all_of(send_g, got_g, 2).wait_send()
     all_of(send_o, got_o, 3).wait_send()
 
 
@@ -295,7 +314,8 @@
     hbm = pl.BlockSpec(memory_space=pltpu.HBM)
     smem = pl.BlockSpec(memory_space=pltpu.SMEM)
     slots = pltpu.VMEM((blocks, group, rows), BF16)
-    lines = pltpu.VMEM((blocks, 1, rows), F32)
+    lines = pltpu.VMEM((blocks, rows), F32)
+    ring = pltpu.VMEM((sizes[0], blocks // sizes[0], rows), BF16)
     owners = (old_owner.reshape(1, blocks), new_owner.reshape(1, blocks))
     arrays = (value_rows, gate_rows, filter_rows, *owners, *tables)
     loaded = [pltpu.VMEM(t.shape, t.dtype) for t in arrays]
@@ -305,7 +325,7 @@
         in_specs=[smem] + [hbm] * len(arrays),
         out_specs=hbm,
         scratch_shapes=[pltpu.VMEM((rows, channels), BF16)] + loaded + [
-            slots, slots, lines, slots, slots, lines, slots, slots,
+            slots, slots, slots, slots, slots, slots, lines, lines, ring, ring,
             pltpu.VMEM((blocks * group, rows), F32),
             pltpu.VMEM((blocks, group * rows), BF16),
             pltpu.VMEM(((group + 1) * blocks, 2 * rows), BF16),
@@ -317,8 +337,8 @@
             pltpu.VMEM((8, blocks), jnp.int32),
             pltpu.SMEM((8, blocks), jnp.int32),
             pltpu.SemaphoreType.DMA((len(arrays) + 5,)),
-            pltpu.SemaphoreType.DMA((5,)),
-            pltpu.SemaphoreType.DMA((5,)),
+            pltpu.SemaphoreType.DMA((6,)),
+            pltpu.SemaphoreType.DMA((6,)),
         ],
         compiler_params=pltpu.CompilerParams(
             collective_id=0, has_side_effects=True, vmem_limit_bytes=64 << 20

time: 61.6 us -> 60.9 us (0.989)
  Pallas kernels: 59.5 us -> 58.8 us
    pallas_call x1, Pallas kernels: 59.5 us -> 58.8 us  [body(): pl.pallas_call(functools.partial(kernel, blocks, group, sizes), out_shape...]
where the time goes in v3:
time: 60.9 us; the launch traced here: 60.7 us
  Pallas kernels  58.8 us (97%)
  local copies, waits for them, and re-layouts  1.88 us (3%)
    pallas_call x1, Pallas kernels, body(): pl.pallas_call(functools.partial(kernel, blocks, group, sizes), out_shape...  58.8 us
    unnamed x1, local copies, waits for them, and re-layouts  1.88 us

profile of v3, /device:TPU:2, one launch (start us, length us, event | category | flops | bytes accessed | tf_op | source)
XLA Modules:
  0.0 60.7 jit_solution(8481141083687170699)
XLA Ops:
  0.0 58.8 %shard_map.118 = bf16[128,2048]{1,0:T(8,128)(2,1)} custom-call(f32[2048]{0:T(1024)} %skip_ref.1, bf16[128,2048]{1,0:T(8,128)(2,1)} %value_hbm.1, bf16[128,2048]{1,0:T(8,128)(2,1)} %gate_hbm.1, bf16[128,128]{1,0:T(8,128)(2,1)} %filter_hbm.1, s32[1,128]{1,0:T(1,128)} %bitcast.2, s32[1,128]{1,0:T(1,128)} %bitcast.3, bf16[256,128]{1,0:T(8,128)(2,1)} %constant.12.clone.first_hbm, ...), custom_call_target="tpu_custom_call" | custom-call | tf_op jit(solution)/shard_map/pallas_call | solution.py:322
  58.8 1.9 %copy.14 = bf16[128,2048]{1,0:T(8,128)(2,1)} copy(bf16[128,2048]{1,0:T(8,128)(2,1)} %shard_map.118) | data formatting | bytes 1048576

commit v4 on v3

--- a/solution.py
+++ b/solution.py
@@ -12,6 +12,7 @@
 MESH = pl.DeviceIdType.MESH
 F32 = jnp.float32
 BF16 = jnp.bfloat16
+PARTS = 4
 
 
 def twist(indices, period):
@@ -67,11 +68,11 @@
     blocks, group, sizes,
     skip_ref, value_hbm, gate_hbm, filter_hbm, old_hbm, new_hbm,
     first_hbm, last_hbm, fwd_hbm, inv_hbm, turn_hbm, edge_hbm,
-    out_hbm, out_ref,
+    mixed_hbm, sums_hbm, partner_hbm, out_ref,
     value_ref, gate_ref, filter_ref, old_ref, new_ref,
     first_ref, last_ref, fwd_ref, inv_ref, turn_ref, edge_ref,
     send_v, send_g, got_v, got_g, send_o, got_o, send_f, got_f, send_f2, got_f2,
-    wide, lanes, turned, back, conv, edges, sums, partner_sums, route_row, route_ref,
+    wide, lanes, turned, back, conv, edges, sums, route_row, route_ref,
     load_sem, send_sem, recv_sem,
 ):
     me = lax.axis_index("ctx")
@@ -111,9 +112,9 @@
 
         def turn_of(i, carry):
             r = low - 1 - i
-            dy = r % ny
-            dx = (r // ny) % nx
-            dc = r // (ny * nx)
+            dc = r % nc
+            dy = (r // nc) % ny
+            dx = r // (ny * nc)
             place = (((y + dy) % ny) * nx + (x + dx) % nx) * nc + (c + dc) % nc
             for dz in steps:
                 act(heights[dz] + place)
@@ -282,28 +283,51 @@
 
     full = got_o[...].astype(F32).reshape(blocks * group, rows)
     sums[...] = jnp.broadcast_to(jnp.sum(full * full, axis=0, keepdims=True), sums.shape)
-    swap = remote(sums, partner_sums, 4, {"dp": 1 - half})
+    swap = remote(sums, partner_hbm, 4, {"dp": 1 - half})
     swap.start()
-    for tile in range(channels // 128):
-        piece = got_o[tile * per_tile:(tile + 1) * per_tile].reshape(128, rows)
-        out_ref[:, tile * 128:(tile + 1) * 128] = transposed(piece).astype(BF16)
-    swap.wait()
-    scale = lax.rsqrt((sums[...] + partner_sums[...]) / (2 * channels) + 1e-05).T[:, 0:1]
+    keep = pltpu.make_async_copy(sums, sums_hbm, load_sem.at[len(loads) + 1])
+    keep.start()
     stores = []
-    for i in range(4):
-        at = slice(i * (channels // 4), (i + 1) * (channels // 4))
-        out_ref[:, at] = (out_ref[:, at].astype(F32) * scale).astype(BF16)
+    for i in range(2):
+        for tile in range(i * channels // 256, (i + 1) * channels // 256):
+            piece = got_o[tile * per_tile:(tile + 1) * per_tile].reshape(128, rows)
+            out_ref[:, tile * 128:(tile + 1) * 128] = transposed(piece).astype(BF16)
+        at = slice(i * channels // 2, (i + 1) * channels // 2)
         stores.append(
-            pltpu.make_async_copy(out_ref.at[:, at], out_hbm.at[:, at], load_sem.at[len(loads) + 1 + i])
+            pltpu.make_async_copy(out_ref.at[:, at], mixed_hbm.at[:, at], load_sem.at[len(loads) + 2 + i])
         )
         stores[-1].start()
+    keep.wait()
     for store in stores:
         store.wait()
+    swap.wait()
     all_of(send_v, got_v, 0).wait_send()
     first_hop.wait_send()
     second_hop.wait_send()
     all_of(send_g, got_g, 2).wait_send()
     all_of(send_o, got_o, 3).wait_send()
+
+
+def scaled(whole, sums_hbm, partner_hbm, mixed_hbm, out_hbm, sums, mixed, out, in_sem, out_sem):
+    rows = mixed.shape[0]
+    part = rows // PARTS
+    parts = [slice(i * part, (i + 1) * part) for i in range(PARTS)]
+    ways = [(sums_hbm, sums.at[0]), (partner_hbm, sums.at[1])]
+    ways += [(mixed_hbm.at[at], mixed.at[at]) for at in parts]
+    loads = [pltpu.make_async_copy(src, dst, in_sem.at[i]) for i, (src, dst) in enumerate(ways)]
+    for load in loads:
+        load.start()
+    for load in loads[:2]:
+        load.wait()
+    scale = lax.rsqrt((sums[0] + sums[1]) / whole + 1e-05).T[:, 0:1]
+    stores = []
+    for i, at in enumerate(parts):
+        loads[2 + i].wait()
+        out[at] = (mixed[at].astype(F32) * scale[at]).astype(BF16)
+        stores.append(pltpu.make_async_copy(out.at[at], out_hbm.at[at], out_sem.at[i]))
+        stores[-1].start()
+    for store in stores:
+        store.wait()
 
 
 def body(sizes, value_rows, gate_rows, filter_rows, skip, old_owner, new_owner):
@@ -319,12 +343,14 @@
     owners = (old_owner.reshape(1, blocks), new_owner.reshape(1, blocks))
     arrays = (value_rows, gate_rows, filter_rows, *owners, *tables)
     loaded = [pltpu.VMEM(t.shape, t.dtype) for t in arrays]
-    return pl.pallas_call(
+    slab = pltpu.VMEM((rows, channels), BF16)
+    sums = jax.ShapeDtypeStruct((8, rows), F32)
+    mixed, own_sums, partner_sums = pl.pallas_call(
         functools.partial(kernel, blocks, group, sizes),
-        out_shape=jax.ShapeDtypeStruct((rows, channels), BF16),
+        out_shape=[jax.ShapeDtypeStruct((rows, channels), BF16), sums, sums],
         in_specs=[smem] + [hbm] * len(arrays),
-        out_specs=hbm,
-        scratch_shapes=[pltpu.VMEM((rows, channels), BF16)] + loaded + [
+        out_specs=[hbm] * 3,
+        scratch_shapes=[slab] + loaded + [
             slots, slots, slots, slots, slots, slots, lines, lines, ring, ring,
             pltpu.VMEM((blocks * group, rows), F32),
             pltpu.VMEM((blocks, group * rows), BF16),
@@ -333,10 +359,9 @@
             pltpu.VMEM((blocks * group, rows), F32),
             pltpu.VMEM((group + 16, rows), F32),
             pltpu.VMEM((8, rows), F32),
-            pltpu.VMEM((8, rows), F32),
             pltpu.VMEM((8, blocks), jnp.int32),
             pltpu.SMEM((8, blocks), jnp.int32),
-            pltpu.SemaphoreType.DMA((len(arrays) + 5,)),
+            pltpu.SemaphoreType.DMA((len(arrays) + 4,)),
             pltpu.SemaphoreType.DMA((6,)),
             pltpu.SemaphoreType.DMA((6,)),
         ],
@@ -344,6 +369,18 @@
             collective_id=0, has_side_effects=True, vmem_limit_bytes=64 << 20
         ),
     )(skip, *arrays)
+    return pl.pallas_call(
+        functools.partial(scaled, channels * lax.axis_size("dp")),
+        out_shape=jax.ShapeDtypeStruct((rows, channels), BF16),
+        in_specs=[hbm] * 3,
+        out_specs=hbm,
+        scratch_shapes=[
+            pltpu.VMEM((2, 8, rows), F32), slab, slab,
+            pltpu.SemaphoreType.DMA((PARTS + 2,)),
+            pltpu.SemaphoreType.DMA((PARTS,)),
+        ],
+        compiler_params=pltpu.CompilerParams(vmem_limit_bytes=64 << 20),
+    )(own_sums, partner_sums, mixed)
 
 
 def solution(mesh):

time: 60.9 us -> 59.8 us (0.982)
  local copies, waits for them, and re-layouts: 1.88 us -> 0 us
  Pallas kernels: 58.8 us -> 59.5 us
    pallas_call x0 -> x1, Pallas kernels: none -> 2 us  [body(): pl.pallas_call(functools.partial(scaled, channels * lax.axis_size('dp')),...]
    unnamed x1 -> x0, local copies, waits for them, and re-layouts: 1.88 us -> none
    pallas_call x1, Pallas kernels: 58.8 us -> 57.5 us  [body(): pl.pallas_call(functools.partial(kernel, blocks, group, sizes), out_shape...]
where the time goes in v4:
time: 59.8 us; the launch traced here: 59.5 us
  Pallas kernels  59.5 us (99%)
    pallas_call x1, Pallas kernels, body(): pl.pallas_call(functools.partial(kernel, blocks, group, sizes), out_shape...  57.5 us
    pallas_call x1, Pallas kernels, body(): pl.pallas_call(functools.partial(scaled, channels * lax.axis_size('dp')),...  2 us

profile of v4, /device:TPU:2, one launch (start us, length us, event | category | flops | bytes accessed | tf_op | source)
XLA Modules:
  0.0 59.5 jit_solution(12289695302313234336)
XLA Ops:
  0.0 57.5 %shard_map.118 = (bf16[128,2048]{1,0:T(8,128)(2,1)}, f32[8,128]{1,0:T(8,128)}, f32[8,128]{1,0:T(8,128)}) custom-call(f32[2048]{0:T(1024)} %skip_ref.1, bf16[128,2048]{1,0:T(8,128)(2,1)} %value_hbm.1, bf16[128,2048]{1,0:T(8,128)(2,1)} %gate_hbm.1, bf16[128,128]{1,0:T(8,128)(2,1)} %filter_hbm.1, s32[1,128]{1,0:T(1,128)} %bitcast.2, s32[1,128]{1,0:T(1,128)} %bitcast.3, ...), custom_call_target="tpu_custom_call" | custom-call | tf_op jit(solution)/shard_map/pallas_call | solution.py:348
  57.5 2.0 %shard_map.119 = bf16[128,2048]{1,0:T(8,128)(2,1)} custom-call(f32[8,128]{1,0:T(8,128)} %get-tuple-element.8.sums_hbm, f32[8,128]{1,0:T(8,128)} %get-tuple-element.9.partner_hbm, bf16[128,2048]{1,0:T(8,128)(2,1)} %get-tuple-element.10.mixed_hbm), custom_call_target="tpu_custom_call" | custom-call | tf_op jit(solution)/shard_map/pallas_call | solution.py:372

commit v5 on v4

--- a/solution.py
+++ b/solution.py
@@ -281,8 +281,12 @@
     each_peer(send_out)
     all_of(send_o, got_o, 3).wait_recv()
 
-    full = got_o[...].astype(F32).reshape(blocks * group, rows)
-    sums[...] = jnp.broadcast_to(jnp.sum(full * full, axis=0, keepdims=True), sums.shape)
+    square_sums = [jnp.zeros((8, rows), F32) for _ in range(4)]
+    for slot in range(0, blocks, 2):
+        pieces = got_o[slot:slot + 2].astype(F32).reshape(4, 8, rows)
+        square_sums = [square_sums[i] + pieces[i] * pieces[i] for i in range(4)]
+    total = square_sums[0] + square_sums[1] + (square_sums[2] + square_sums[3])
+    sums[...] = jnp.broadcast_to(jnp.sum(total, axis=0, keepdims=True), sums.shape)
     swap = remote(sums, partner_hbm, 4, {"dp": 1 - half})
     swap.start()
     keep = pltpu.make_async_copy(sums, sums_hbm, load_sem.at[len(loads) + 1])

time: 59.8 us -> 59.5 us (level)
  no operation moved by 1% of the time
where the time goes in v5:
time: 59.5 us; the launch traced here: 59.3 us
  Pallas kernels  59.3 us (100%)
    pallas_call x1, Pallas kernels, body(): pl.pallas_call(functools.partial(kernel, blocks, group, sizes), out_shape...  57.3 us
    pallas_call x1, Pallas kernels, body(): pl.pallas_call(functools.partial(scaled, channels * lax.axis_size('dp')),...  2 us

profile of v5, /device:TPU:2, one launch (start us, length us, event | category | flops | bytes accessed | tf_op | source)
XLA Modules:
  0.0 59.3 jit_solution(9785259892810925163)
XLA Ops:
  0.0 57.3 %shard_map.118 = (bf16[128,2048]{1,0:T(8,128)(2,1)}, f32[8,128]{1,0:T(8,128)}, f32[8,128]{1,0:T(8,128)}) custom-call(f32[2048]{0:T(1024)} %skip_ref.1, bf16[128,2048]{1,0:T(8,128)(2,1)} %value_hbm.1, bf16[128,2048]{1,0:T(8,128)(2,1)} %gate_hbm.1, bf16[128,128]{1,0:T(8,128)(2,1)} %filter_hbm.1, s32[1,128]{1,0:T(1,128)} %bitcast.2, s32[1,128]{1,0:T(1,128)} %bitcast.3, ...), custom_call_target="tpu_custom_call" | custom-call | tf_op jit(solution)/shard_map/pallas_call | solution.py:352
  57.3 2.0 %shard_map.119 = bf16[128,2048]{1,0:T(8,128)(2,1)} custom-call(f32[8,128]{1,0:T(8,128)} %get-tuple-element.8.sums_hbm, f32[8,128]{1,0:T(8,128)} %get-tuple-element.9.partner_hbm, bf16[128,2048]{1,0:T(8,128)(2,1)} %get-tuple-element.10.mixed_hbm), custom_call_target="tpu_custom_call" | custom-call | tf_op jit(solution)/shard_map/pallas_call | solution.py:376

commit v6 on v5

--- a/solution.py
+++ b/solution.py
@@ -97,11 +97,12 @@
 
     def greet(k, carry):
         pl.semaphore_signal(
-            barrier, inc=1, device_id={"ctx": lax.rem(me + k, blocks)}, device_id_type=MESH
+            barrier, inc=1, device_id={"ctx": lax.rem(me + blocks // 2 + blocks - k, blocks)}, device_id_type=MESH
         )
         return carry
 
-    lax.fori_loop(1, blocks, greet, 0, unroll=8)
+    lax.fori_loop(0, blocks // 2, greet, 0, unroll=8)
+    lax.fori_loop(blocks // 2 + 1, blocks, greet, 0, unroll=8)
     pl.semaphore_signal(barrier, inc=1, device_id={"dp": 1 - half}, device_id_type=MESH)
 
     z, y, x, c = me // low, (me // (nx * nc)) % ny, (me // nc) % nx, me % nc

time: 59.5 us -> 59.7 us (level)
  no operation moved by 1% of the time
where the time goes in v6:
time: 59.7 us; the launch traced here: 59.5 us
  Pallas kernels  59.5 us (100%)
    pallas_call x1, Pallas kernels, body(): pl.pallas_call(functools.partial(kernel, blocks, group, sizes), out_shape...  57.5 us
    pallas_call x1, Pallas kernels, body(): pl.pallas_call(functools.partial(scaled, channels * lax.axis_size('dp')),...  2 us

profile of v6, /device:TPU:2, one launch (start us, length us, event | category | flops | bytes accessed | tf_op | source)
XLA Modules:
  0.0 59.5 jit_solution(4496776958275107506)
XLA Ops:
  0.0 57.5 %shard_map.118 = (bf16[128,2048]{1,0:T(8,128)(2,1)}, f32[8,128]{1,0:T(8,128)}, f32[8,128]{1,0:T(8,128)}) custom-call(f32[2048]{0:T(1024)} %skip_ref.1, bf16[128,2048]{1,0:T(8,128)(2,1)} %value_hbm.1, bf16[128,2048]{1,0:T(8,128)(2,1)} %gate_hbm.1, bf16[128,128]{1,0:T(8,128)(2,1)} %filter_hbm.1, s32[1,128]{1,0:T(1,128)} %bitcast.2, s32[1,128]{1,0:T(1,128)} %bitcast.3, ...), custom_call_target="tpu_custom_call" | custom-call | tf_op jit(solution)/shard_map/pallas_call | solution.py:353
  57.5 2.0 %shard_map.119 = bf16[128,2048]{1,0:T(8,128)(2,1)} custom-call(f32[8,128]{1,0:T(8,128)} %get-tuple-element.8.sums_hbm, f32[8,128]{1,0:T(8,128)} %get-tuple-element.9.partner_hbm, bf16[128,2048]{1,0:T(8,128)(2,1)} %get-tuple-element.10.mixed_hbm), custom_call_target="tpu_custom_call" | custom-call | tf_op jit(solution)/shard_map/pallas_call | solution.py:377
